TPU v7x, 256 devices: a whole 4x4x8 slice. The times are simulated.
256 devices in a mesh: ref: 64 (over z, y_lo, x), win: 4 (over y_hi, core).
Axes of the slice: x: 4, y: 4 (y_hi: 2, y_lo: 2; y = y_hi * 2 + y_lo), z: 8, core: 2. Of those that a mesh axis runs over, the one named last changes fastest.
Arguments:
- queries: bfloat16 [2048, 8192], P('ref', 'win'), may hold values from -1 to 1, as said below
- references: bfloat16 [65536, 8192], P('ref', 'win'), may hold values from -1 to 1, as said below
- labels: int32 [512], P('ref'), may hold values from 0 to 7, as said below
- kernel: float32 [9, 8], replicated, may hold values from 0.02 to 0.3
- class_bias: float32 [8], replicated, may hold values from -4 to 4
Outputs:
- ancestry_logprob: float32 [16, 8, 2048], P('win', None, 'ref')
Inputs may be any that keep to these rules, and one draw needn't show every extreme that they name: `queries`: every entry is -1 or +1. `references`: every entry is -1 or +1. Every ancestry labels at least one block.
All inputs are finite; a program needn't handle non-finite values.
Results may differ from a plain program's by a relative error of at most 0.0003.
Values may be sent and summed in bfloat16 or wider, within the bound.
A program may use at most 64 MiB of HBM per device.

v0:
```python
import jax
import jax.numpy as jnp
from jax import lax
from jax.sharding import PartitionSpec as P

S = 512
A = 8
BLOCK = 128
TAPS = 9


neg_floor = -1e30


def combined_all(shard, axis, combine):
    everything = lax.all_gather(shard, axis)
    leading = everything[0]

    def lap(k, so_far):
        return combine(so_far, everything[k])

    return lax.fori_loop(1, lax.axis_size(axis), lap, leading)


def with_halo(block, sides, width):
    for axis, dim in sides:
        count = lax.axis_size(axis)
        forward = [(i, i + 1) for i in range(count - 1)]
        backward = [(target, source) for source, target in forward]
        low = lax.ppermute(
            lax.slice_in_dim(block, block.shape[dim] - width, None, axis=dim), axis, forward
        )
        high = lax.ppermute(lax.slice_in_dim(block, 0, width, axis=dim), axis, backward)
        block = jnp.concatenate([low, block, high], axis=dim)
    return block


def pool_rows(query_piece, references, member, windows):
    score_scale = 256.0 / S
    row_count = query_piece.shape[0]
    block_count = references.shape[0] // BLOCK
    results = []
    for window in range(windows):
        query_part = query_piece[:, window * S : (window + 1) * S]
        ref_part = references[:, window * S : (window + 1) * S]
        scores = (
            jnp.einsum("qs,rs->qr", query_part, ref_part, preferred_element_type=jnp.float32)
            * score_scale
        )
        blocks = scores.reshape(row_count, block_count, BLOCK)
        block_peak = jnp.max(blocks, axis=2)
        block_total = jnp.sum(jnp.exp(blocks - block_peak[:, :, None]), axis=2)
        group_peak = jnp.max(jnp.where(member[None], block_peak[:, :, None], neg_floor), axis=1)
        weights = jnp.where(
            member[None],
            block_total[:, :, None] * jnp.exp(block_peak[:, :, None] - group_peak[:, None, :]),
            0.0,
        )
        group_total = jnp.sum(weights, axis=1)
        group_lse = jnp.where(group_total > 0, group_peak + jnp.log(group_total), neg_floor)
        results.append(group_lse.T)
    return jnp.stack(results)


def combine_lse(left_part, right_part):
    higher = jnp.maximum(left_part, right_part)
    return higher + jnp.log(jnp.exp(left_part - higher) + jnp.exp(right_part - higher))


def per_device(queries, references, labels, kernel, class_bias):
    member = labels[:, None] == jnp.arange(A, dtype=jnp.int32)[None, :]
    windows = references.shape[1] // S
    query_count = queries.shape[0]
    partial_value = pool_rows(
        lax.all_gather(queries, "ref", axis=0, tiled=True), references, member, windows
    )
    owner_start = lax.axis_index("ref") * query_count
    combined = combined_all(partial_value, "ref", combine_lse)
    pooled = lax.dynamic_slice_in_dim(combined, owner_start, query_count, 2)
    centered = pooled - jnp.mean(pooled, axis=1, keepdims=True)
    padded = with_halo(centered, (("win", 0),), TAPS // 2)
    smoothed = jnp.zeros_like(centered)
    for offset in range(TAPS):
        smoothed = smoothed + kernel[offset][None, :, None] * padded[offset : offset + windows]
    logits = smoothed + class_bias[None, :, None]
    return jax.nn.log_softmax(logits, axis=1)


def solution(mesh):
    in_specs = (P("ref", "win"), P("ref", "win"), P("ref"), P(), P())
    out_specs = P("win", None, "ref")
    return jax.shard_map(
        per_device, mesh=mesh, in_specs=in_specs, out_specs=out_specs, check_vma=False
    )
```

profile of v0, /device:TPU:1, one launch (start us, length us, event | category | flops | bytes accessed | tf_op | source)
XLA Modules:
  0.0 767.0 jit_solution(14383319232930999667)
XLA Ops:
  8.0 275.9 %all-gather.4.cloned.1.call-done = bf16[2048,2048]{1,0:T(8,128)(2,1)} async-done(((bf16[32,2048]{1,0:T(8,128)(2,1)}), bf16[2048,2048]{1,0:T(8,128)(2,1)}) %all-gather.4.cloned.1.call-update) | async-done | bytes 8388624 | tf_op jit(solution)/shard_map/all_gather | solution.py:75
  283.9 4.4 bitcast_reduce_fusion.3
  288.3 1.5 fusion.15
  289.9 1.8 copy-done.1
  291.7 2.4 bitcast_reduce_fusion
  294.1 1.5 fusion.9
  295.6 2.4 bitcast_reduce_fusion.1
  298.0 1.5 fusion.11
  299.5 2.6 bitcast_reduce_fusion.2
  302.1 1.5 fusion.13
  305.1 331.1 %all-gather.6.cloned.1.call-done = f32[256,8,2048]{2,1,0:T(8,128)} async-done(((f32[4,8,2048]{2,1,0:T(8,128)}), f32[256,8,2048]{2,1,0:T(8,128)}) %all-gather.6.cloned.1.call-update) | async-done | bytes 16777232 | tf_op jit(solution)/shard_map/all_gather | solution.py:16
  637.2 76.0 %while.15 = (s32[]{:T(128)}, f32[4,8,2048]{2,1,0:T(8,128)S(1)}, f32[64,4,8,2048]{3,2,1,0:T(8,128)}, s32[]{:T(128)}, s32[]{:T(128)}, /*index=5*/s32[]{:T(128)}) while((s32[]{:T(128)}, f32[4,8,2048]{2,1,0:T(8,128)S(1)}, f32[64,4,8,2048]{3,2,1,0:T(8,128)}, s32[]{:T(128)}, s32[]{:T(128)}, /*index=5*/s32[]{:T(128)}) %tuple.62), condition=%wide.region_17.18_spmd, body=%wide.region_16.17_spmd.sunk | while | flops 327685 | bytes 786539 | solution.py:22
  637.2 1.2 fusion.53
  638.4 1.2 fusion.53
  639.6 1.2 fusion.53
  640.8 1.2 fusion.53
  642.0 1.2 fusion.53
  643.2 1.2 fusion.53
  644.4 1.2 fusion.53
  645.6 1.2 fusion.53
  646.8 1.2 fusion.53
  648.0 1.2 fusion.53
  649.2 1.2 fusion.53
  650.4 1.2 fusion.53
  651.6 1.2 fusion.53
  652.9 1.2 fusion.53
  654.1 1.2 fusion.53
  655.3 1.2 fusion.53
  656.5 1.2 fusion.53
  657.7 1.2 fusion.53
  658.9 1.2 fusion.53
  660.1 1.2 fusion.53
  661.3 1.2 fusion.53
  662.5 1.2 fusion.53
  663.7 1.2 fusion.53
  664.9 1.2 fusion.53
  666.1 1.2 fusion.53
  667.3 1.2 fusion.53
  668.5 1.2 fusion.53
  669.7 1.2 fusion.53
  670.9 1.2 fusion.53
  672.1 1.2 fusion.53
  673.4 1.2 fusion.53
  674.6 1.2 fusion.53
  675.8 1.2 fusion.53
  677.0 1.2 fusion.53
  678.2 1.2 fusion.53
  679.4 1.2 fusion.53
  680.6 1.2 fusion.53
  681.8 1.2 fusion.53
  683.0 1.2 fusion.53
  684.2 1.2 fusion.53
  686.6 1.2 fusion.53
  690.2 1.2 fusion.53
  692.6 1.2 fusion.53
  695.1 1.2 fusion.53
  697.5 1.2 fusion.53
  699.9 1.2 fusion.53
  702.3 1.2 fusion.53
  704.7 1.2 fusion.53
  707.1 1.2 fusion.53
  709.5 1.2 fusion.53
  713.3 41.3 %collective-permute-start.1 = (f32[4,8,32]{2,1,0:T(8,128)S(1)}, f32[4,8,32]{2,1,0:T(8,128)S(1)}, u32[]{:S(2)}, u32[]{:S(2)}) collective-permute-start(f32[4,8,32]{2,1,0:T(8,128)S(1)} %dynamic-slice_subtract_fusion), channel_id=1, source_target_pairs={{1,0},{2,1},{3,2},{5,4},{6,5},{7,6},{9,8},{10,9},{11,10},{13,12},{... | collective-permute-start | bytes 12296 | tf_op jit(solution)/shard_map/ppermute | solution.py:33
  754.6 4.0 collective-permute-start
  (40 shorter events, 21.2 us)
Async XLA Ops:
  6.5 277.4 %all-gather.4.cloned.1.call-start = ((), (), s32[]{:S(2)}) async-start(), calls=%async_computation | async-start | bytes 8519680 | tf_op jit(solution)/shard_map/all_gather | solution.py:75
  7.3 628.9 %all-gather.6.cloned.1.call-start = ((), (), s32[]{:S(2)}) async-start(), calls=%async_computation.1 | async-start | bytes 17039360 | tf_op jit(solution)/shard_map/all_gather | solution.py:16
  283.9 6.0 copy-start.2
  288.3 3.4 copy-start.1
  302.1 456.5 %copy-start = (f32[9,8]{0,1:T(8,128)S(1)}, f32[9,8]{0,1:T(8,128)}, u32[]{:S(2)}) copy-start(f32[9,8]{0,1:T(8,128)} %param.10) | copy-start | bytes 868
  302.1 457.3 %copy-start.3 = (f32[8]{0:T(128)S(1)}, f32[8]{0:T(128)}, u32[]{:S(2)}) copy-start(f32[8]{0:T(128)} %param.11) | copy-start | bytes 100
  713.3 45.6 %collective-permute-start.1 = (f32[4,8,32]{2,1,0:T(8,128)S(1)}, f32[4,8,32]{2,1,0:T(8,128)S(1)}, u32[]{:S(2)}, u32[]{:S(2)}) collective-permute-start(f32[4,8,32]{2,1,0:T(8,128)S(1)} %dynamic-slice_subtract_fusion), channel_id=1, source_target_pairs={{1,0},{2,1},{3,2},{5,4},{6,5},{7,6},{9,8},{10,9},{11,10},{13,12},{... | collective-permute-start | bytes 12296 | tf_op jit(solution)/shard_map/ppermute | solution.py:33
  754.6 4.8 collective-permute-start
Sparse Core Ops, SparseCore 0:
  9.1 274.7 all-gather.3
  305.2 330.9 all-gather.5
where the time goes:
time: 769 us; the launch traced here: 767 us
  waiting for transfers between devices  608 us (79%)
  other arithmetic  83.8 us (11%)
  starting transfers between devices  45.3 us (6%)
  between operations  13.6 us (2%)
  matrix products  11.8 us (2%)
    all_gather x1, waiting for transfers between devices, combined_all(): everything = lax.all_gather(shard, axis)  331 us
    all_gather x1, waiting for transfers between devices, per_device(): lax.all_gather(queries, 'ref', axis=0, tiled=True)  276 us
    add x63, other arithmetic, combine_lse(): higher + jnp.log(jnp.exp(left_part - higher) + jnp.exp(right_part - higher))  74.7 us
    ppermute x1, starting transfers between devices, with_halo(): lax.ppermute(lax.slice_in_dim(block, 0, width, axis=dim), axis, backward)  41.3 us
  transfers between devices with their start and end apart: 4, of which 3 were waited for; matrix products, arithmetic and copies ran while one was open for 0% of the time, Pallas kernels for 0%

commit v1 on v0

v1 whole, which is shorter than its diff:
```python
import functools

import jax
import jax.numpy as jnp
from jax import lax
from jax.experimental import pallas as pl
from jax.experimental.pallas import tpu as pltpu
from jax.sharding import PartitionSpec as P

S = 512
A = 8
BLOCK = 128
TAPS = 9
NX, NY, NZ = 4, 2, 8
ROWS = 32
WIN = 4
REFS = 1024
NB = REFS // BLOCK
PLANE = NX * NY
LANES = WIN * ROWS
FLOOR = -1e30
MESH = pl.DeviceIdType.MESH


class Ids:
    def __init__(self):
        self.numbers = {}

    def __call__(self, *name):
        return self.numbers.setdefault(name, len(self.numbers))


def lse(values):
    peak = functools.reduce(jnp.maximum, values)
    total = functools.reduce(jnp.add, [jnp.exp(v - peak) for v in values])
    return peak + jnp.log(total)


def body(ids, q_ref, r_ref, lab_ref, ker_ref, bias_ref, out_ref,
         g, refs, pen, part, sbuf, r1, zbuf, r2, cent, halo, ssem, rsem, lsem):
    ref = lax.axis_index("ref")
    win = lax.axis_index("win")
    z, y, x = ref // PLANE, (ref // NX) % NY, ref % NX
    ny = 1 - y

    def at(zz, yy, xx):
        return {"ref": zz * PLANE + yy * NX + xx}

    def zz(delta):
        return (z + delta + NZ) % NZ

    def xx(delta):
        return (x + delta + NX) % NX

    local = []
    for w in range(WIN):
        local.append(pltpu.make_async_copy(
            q_ref.at[:, pl.ds(w * S, S)], g.at[w, z, y, x], lsem.at[w]))
    for w in range(WIN):
        local.append(pltpu.make_async_copy(
            r_ref.at[:, pl.ds(w * S, S)], refs.at[w], lsem.at[WIN + w]))
    for copy in local:
        copy.start()

    barrier = pltpu.get_barrier_semaphore()
    peers = [at(z, (y + dy) % NY, xx(dx)) for dy in range(NY) for dx in range(NX) if dy or dx]
    peers += [at(zz(d), y, x) for d in range(1, NZ)]
    peers += [{"win": (win + 1) % WIN}, {"win": (win + WIN - 1) % WIN}]
    for peer in peers:
        pl.semaphore_signal(barrier, inc=1, device_id=peer, device_id_type=MESH)

    ancestry = lax.broadcasted_iota(jnp.int32, (A, 2 * LANES), 0)
    for b in range(NB):
        pen[b] = jnp.where(ancestry == lab_ref[b], 0.0, FLOOR)

    pl.semaphore_wait(barrier, len(peers))
    for copy in local[:WIN]:
        copy.wait()

    sent = []

    def copy_of(name, src, dst, device):
        n = ids(*name)
        return pltpu.make_async_remote_copy(
            src_ref=src, dst_ref=dst, send_sem=ssem.at[n], recv_sem=rsem.at[n],
            device_id=device, device_id_type=MESH)

    def send(name, src, device, dst=None):
        copy = copy_of(name, src, src if dst is None else dst, device)
        copy.start()
        sent.append(copy)

    def recv(name, dst):
        copy_of(name, dst, dst, at(z, ny, x)).wait_recv()

    right, left = at(z, y, xx(1)), at(z, y, xx(-1))
    other = at(z, ny, x)
    down = {1: at(zz(-1), y, x), -1: at(zz(1), y, x)}
    signs = (1, -1)
    two = pl.ds(0, 2)
    ad, bb = pl.ds(0, 2), pl.ds(2, 2)
    both = pl.ds(0, NY)

    own = g.at[pl.ds(0, WIN), z, y, x]
    send(("x0", 0), g.at[ad, z, y, x], right)
    send(("x0", 1), g.at[ad, z, y, x], left)
    send(("y0", 0), own, other)
    for s in signs:
        send(("z1", s, 0), own, down[s])

    def x_stage(zb):
        def start():
            send(("bx", zb, 0), g.at[bb, zz(zb), both, x], right)
            send(("bx", zb, 1), g.at[bb, zz(zb), both, x], left)

        def forward():
            recv(("bx", zb, 0), g.at[bb, zz(zb), both, xx(-1)])
            send(("bf", zb, 0), g.at[2, zz(zb), both, xx(-1)], right)
            recv(("bx", zb, 1), g.at[bb, zz(zb), both, xx(1)])
            send(("bf", zb, 1), g.at[3, zz(zb), both, xx(1)], left)

        def finish():
            recv(("bf", zb, 0), g.at[2, zz(zb), both, xx(2)])
            recv(("bf", zb, 1), g.at[3, zz(zb), both, xx(2)])

        return start, forward, finish

    def y_start(zb):
        send(("dy", zb), g.at[1, zz(zb), y], other)

    def y_finish(zb):
        recv(("dy", zb), g.at[1, zz(zb), ny])

    stages = {zb: x_stage(zb) for zb in (0, 1, -1, 2, -2, 3, -3, 4)}

    recv(("y0", 0), g.at[pl.ds(0, WIN), z, ny, x])
    for s in signs:
        send(("z1", s, 1), g.at[bb, z, ny, x], down[s])
    recv(("x0", 0), g.at[ad, z, y, xx(-1)])
    send(("xf", 0), g.at[0, z, y, xx(-1)], right)
    recv(("x0", 1), g.at[ad, z, y, xx(1)])
    send(("xf", 1), g.at[1, z, y, xx(1)], left)
    stages[0][0]()
    for n, dx in ((1, -1), (2, 1)):
        send(("y0", n), g.at[ad, z, y, xx(dx)], other)
        for s in signs:
            send(("z1", s, 1 + n), g.at[ad, z, y, xx(dx)], down[s])
    recv(("xf", 0), g.at[0, z, y, xx(2)])
    recv(("xf", 1), g.at[1, z, y, xx(2)])
    send(("y0", 3), g.at[ad, z, y, xx(2)], other)
    for s in signs:
        send(("z1", s, 4), g.at[ad, z, y, xx(2)], down[s])
    for n, dx in ((1, -1), (2, 1), (3, 2)):
        recv(("y0", n), g.at[ad, z, ny, xx(dx)])
    for s in signs:
        send(("z1", s, 5), g.at[0, z, ny], down[s])

    def b_part(k, s):
        zb = zz(s * k)
        if k < 4:
            return g.at[bb, zb, both, x]
        return g.at[2 if s == 1 else 3, zb, both, x]

    def d_part(k, s):
        zb = zz(s * k)
        if k < 4:
            return g.at[1, zb, y]
        return g.at[1, zb, y, pl.ds(0 if s == 1 else 2, 2)]

    def a_part(k, s):
        zb = zz(s * k)
        if k < 4:
            return g.at[0, zb]
        return g.at[0, zb, 0 if s == 1 else 1]

    parts = {"b": b_part, "d": d_part, "a": a_part}

    def pass_on(kind, k, s):
        zb = zz(s * (k - 1))
        if kind == "b":
            src = g.at[bb, zb, both, x] if k < 4 else g.at[2 if s == 1 else 3, zb, both, x]
        elif kind == "d":
            src = g.at[1, zb, y] if k < 4 else g.at[1, zb, y, pl.ds(0 if s == 1 else 2, 2)]
        else:
            src = g.at[0, zb] if k < 4 else g.at[0, zb, 0 if s == 1 else 1]
        send((kind, k, s), src, down[s])

    def take(kind, k, s):
        recv((kind, k, s), parts[kind](k, s))

    def score(w, zb, slot):
        queries = g[w, zb].reshape(2 * LANES, S)
        peaks, totals = [], []
        for b in range(NB):
            scores = lax.dot_general(
                refs[w, b * BLOCK:(b + 1) * BLOCK, :], queries, (((1,), (1,)), ((), ())),
                preferred_element_type=jnp.float32)
            peak = jnp.max(scores, axis=0, keepdims=True)
            totals.append(jnp.sum(jnp.exp((scores - peak) * (256.0 / S)), axis=0, keepdims=True))
            peaks.append(peak * (256.0 / S))
        shifted = [peaks[b] + pen[b] for b in range(NB)]
        top = functools.reduce(jnp.maximum, shifted)
        total = functools.reduce(
            jnp.add, [totals[b] * jnp.exp(shifted[b] - top) for b in range(NB)])
        part[slot, w] = top + jnp.log(total)

    def blocks_of(k):
        return (0,) if k == 0 else (4,) if k == 4 else (k, -k)

    def compute(k, w_from, w_to):
        n = w_to - w_from
        count = len(blocks_of(k))

        def one(i, carry):
            slot, w = i // n, w_from + i % n
            zb = zz(k * (1 - 2 * slot))
            score(w, zb, slot)
            return carry

        lax.fori_loop(0, n * count, one, 0)

    lane = lax.broadcasted_iota(jnp.int32, (A, LANES), 1) // ROWS

    def plane_send(k):
        count = len(blocks_of(k))
        for slot in range(count):
            for o in range(PLANE):
                half = pl.ds((o // WIN) * LANES, LANES)
                packed = None
                for w in range(WIN):
                    shift = ((w - o) % WIN) * ROWS
                    piece = part[slot, w, :, half]
                    piece = pltpu.roll(piece, shift, 1) if shift else piece
                    packed = piece if packed is None else jnp.where(lane == w, piece, packed)
                sbuf[k, o, slot] = packed
        span = pl.ds(0, count)
        for dy in range(NY):
            for dx in range(NX):
                if dy or dx:
                    ty, tx = (y + dy) % NY, xx(dx)
                    send(("p", k, dy, dx), sbuf.at[k, ty * NX + tx, span], at(z, ty, tx),
                         r1.at[k, dy * NX + dx, span])

    def plane_combine(k):
        count = len(blocks_of(k))
        span = pl.ds(0, count)
        for dy in range(NY):
            for dx in range(NX):
                if dy or dx:
                    recv(("p", k, dy, dx), r1.at[k, dy * NX + dx, span])
        for slot, zb in enumerate(blocks_of(k)):
            mine = lse([sbuf[k, y * NX + x, slot]] + [r1[k, n, slot] for n in range(1, PLANE)])
            n = zb % NZ
            zbuf[n] = mine
            if zb:
                send(("r", n), zbuf.at[n], at(zz(zb), y, x), r2.at[n])

    for s in signs:
        recv(("z1", s, 0), g.at[pl.ds(0, WIN), zz(s), y, x])
        recv(("z1", s, 1), g.at[bb, zz(s), ny, x])
        pass_on("b", 2, s)
        stages[s][0]()
    for s in signs:
        for n, dx in ((2, -1), (3, 1), (4, 2)):
            recv(("z1", s, n), g.at[ad, zz(s), y, xx(dx)])
        pass_on("d", 2, s)
        y_start(s)
    for copy in local[WIN:]:
        copy.wait()
    stages[0][1]()
    compute(0, 0, 2)
    for s in signs:
        recv(("z1", s, 5), g.at[0, zz(s), ny])
        pass_on("a", 2, s)
    stages[0][2]()
    compute(0, 2, 4)
    plane_send(0)
    for s in signs:
        stages[s][1]()

    for k in (2, 3):
        for s in signs:
            take("b", k, s)
            pass_on("b", k + 1, s)
            stages[s * k][0]()
        for s in signs:
            take("d", k, s)
            pass_on("d", k + 1, s)
            y_start(s * k)
        for s in signs:
            y_finish(s * (k - 1))
            stages[s * (k - 1)][2]()
        compute(k - 1, 0, 4)
        plane_send(k - 1)
        for s in signs:
            take("a", k, s)
            pass_on("a", k + 1, s)
        for s in signs:
            stages[s * k][1]()
        plane_combine(k - 2)

    for s in signs:
        take("b", 4, s)
    stages[4][0]()
    for s in signs:
        take("d", 4, s)
    y_start(4)
    for s in signs:
        y_finish(s * 3)
        stages[s * 3][2]()
    compute(3, 0, 4)
    plane_send(3)
    stages[4][1]()
    plane_combine(2)
    for s in signs:
        take("a", 4, s)
    y_finish(4)
    compute(4, 0, 2)
    stages[4][2]()
    compute(4, 2, 4)
    plane_send(4)
    plane_combine(3)
    plane_combine(4)

    for n in range(1, NZ):
        recv(("r", n), r2.at[n])
    pooled = lse([zbuf[0]] + [r2[n] for n in range(1, NZ)])
    centered = pooled - jnp.mean(pooled, axis=0, keepdims=True)
    cent[...] = centered
    send(("h", 0), cent, {"win": (win + 1) % WIN}, halo.at[0])
    send(("h", 1), cent, {"win": (win + WIN - 1) % WIN}, halo.at[1])

    def column(read):
        rows = lax.broadcasted_iota(jnp.int32, (A, LANES), 0)
        value = jnp.full((A, LANES), read(0), jnp.float32)
        for a in range(1, A):
            value = jnp.where(rows == a, read(a), value)
        return value

    taps = [column(lambda a, t=t: ker_ref[t, a]) for t in range(TAPS)]
    bias = column(lambda a: bias_ref[a])
    recv(("h", 0), halo.at[0])
    recv(("h", 1), halo.at[1])
    low = jnp.where(win > 0, halo[0], 0.0)
    high = jnp.where(win < WIN - 1, halo[1], 0.0)
    logits = bias
    for t in range(TAPS):
        d = t - TAPS // 2
        if d == 0:
            moved = centered
        elif d < 0:
            shift = (-d * ROWS) % LANES
            moved = low if not shift else jnp.where(
                lane < -d, pltpu.roll(low, shift, 1), pltpu.roll(centered, shift, 1))
        else:
            shift = (-d * ROWS) % LANES
            moved = high if not shift else jnp.where(
                lane >= WIN - d, pltpu.roll(high, shift, 1), pltpu.roll(centered, shift, 1))
        logits = logits + taps[t] * moved
    peak = jnp.max(logits, axis=0, keepdims=True)
    result = logits - peak - jnp.log(jnp.sum(jnp.exp(logits - peak), axis=0, keepdims=True))
    for w in range(WIN):
        out_ref[w] = result[:, w * ROWS:(w + 1) * ROWS]

    for copy in sent:
        copy.wait_send()


MESSAGES = 160


def per_device(queries, references, labels, kernel, class_bias):
    ids = Ids()
    hbm = pl.BlockSpec(memory_space=pl.ANY)
    smem = pl.BlockSpec(memory_space=pltpu.SMEM)
    return pl.pallas_call(
        functools.partial(body, ids),
        out_shape=jax.ShapeDtypeStruct((WIN, A, ROWS), jnp.float32),
        in_specs=[hbm, hbm, smem, smem, smem],
        out_specs=pl.BlockSpec(memory_space=pltpu.VMEM),
        scratch_shapes=[
            pltpu.VMEM((WIN, NZ, NY, NX, ROWS, S), jnp.bfloat16),
            pltpu.VMEM((WIN, REFS, S), jnp.bfloat16),
            pltpu.VMEM((NB, A, 2 * LANES), jnp.float32),
            pltpu.VMEM((2, WIN, A, 2 * LANES), jnp.float32),
            pltpu.VMEM((5, PLANE, 2, A, LANES), jnp.float32),
            pltpu.VMEM((5, PLANE, 2, A, LANES), jnp.float32),
            pltpu.VMEM((NZ, A, LANES), jnp.float32),
            pltpu.VMEM((NZ, A, LANES), jnp.float32),
            pltpu.VMEM((A, LANES), jnp.float32),
            pltpu.VMEM((2, A, LANES), jnp.float32),
            pltpu.SemaphoreType.DMA((MESSAGES,)),
            pltpu.SemaphoreType.DMA((MESSAGES,)),
            pltpu.SemaphoreType.DMA((2 * WIN,)),
        ],
        compiler_params=pltpu.CompilerParams(
            collective_id=0, has_side_effects=True, vmem_limit_bytes=48 * 1024 * 1024),
        cost_estimate=pl.CostEstimate(
            flops=2 * 2048 * REFS * S * WIN, bytes_accessed=5 * 1024 * 1024,
            transcendentals=2048 * REFS * WIN),
    )(queries, references, labels, kernel, class_bias)


def solution(mesh):
    in_specs = (P("ref", "win"), P("ref", "win"), P("ref"), P(), P())
    out_specs = P("win", None, "ref")
    return jax.shard_map(
        per_device, mesh=mesh, in_specs=in_specs, out_specs=out_specs, check_vma=False
    )
```

time: 769 us -> 96.2 us (0.13)
  waiting for transfers between devices: 608 us -> 0 us
  Pallas kernels: 0 us -> 90.3 us
  other arithmetic: 83.8 us -> 0 us
  starting transfers between devices: 45.3 us -> 0 us
  between operations: 13.6 us -> 0.01 us
  matrix products: 11.8 us -> 0 us
    all_gather x2 -> x0, waiting for transfers between devices: 607 us -> none  [the longest x1 331 us: combined_all(): everything = lax.all_gather(shard, axis)]
    pallas_call x0 -> x1, Pallas kernels: none -> 90.3 us  [per_device(): pl.pallas_call(functools.partial(body, ids), out_shape=jax.ShapeDtypeStru...]
    add x63 -> x0, other arithmetic: 74.7 us -> none  [combine_lse(): higher + jnp.log(jnp.exp(left_part - higher) + jnp.exp(right_part - higher))]
    ppermute x2 -> x0, starting transfers between devices: 45.2 us -> none  [the longest x1 41.3 us: with_halo(): lax.ppermute(lax.slice_in_dim(block, 0, width, axis=dim), axis, backward)]
    dot_general x4 -> x0, matrix products: 11.8 us -> none  [pool_rows(): jnp.einsum('qs,rs->qr', query_part, ref_part, preferred_element_type=jnp....]
  transfers between devices with their start and end apart: 4 -> 0, of which waited for: 3 -> 0; matrix products, arithmetic and copies ran while one was open for 0% -> 0% of each run, Pallas kernels for 0% -> 0%
where the time goes in v1:
time: 96.2 us; the launch traced here: 96.1 us
  Pallas kernels  90.3 us (94%)
  local copies, waits for them, and re-layouts  5.78 us (6%)
    pallas_call x1, Pallas kernels, per_device(): pl.pallas_call(functools.partial(body, ids), out_shape=jax.ShapeDtypeStru...  90.3 us
    unnamed x10, local copies, waits for them, and re-layouts  5.78 us

profile of v1, /device:TPU:1, one launch (start us, length us, event | category | flops | bytes accessed | tf_op | source)
XLA Modules:
  0.0 96.1 jit_solution(952358705772172454)
XLA Ops:
  0.0 0.8 copy.6.ker_ref
  0.8 0.0 copy-start
  0.8 2.2 %copy-done = bf16[1024,2048]{1,0:T(8,128)(2,1)S(1)} copy-done((bf16[1024,2048]{1,0:T(8,128)(2,1)S(1)}, bf16[1024,2048]{1,0:T(8,128)(2,1)}, u32[]{:S(2)}) %copy-start) | copy-done | bytes 4194328
  3.0 0.0 copy-start.1
  3.0 0.9 copy-done.1
  3.9 0.0 copy-start.2
  3.9 0.7 copy-done.2
  4.5 0.0 copy-start.3
  4.5 0.7 copy-done.3
  5.2 90.3 %shard_map.55 = f32[4,8,32]{2,1,0:T(8,128)S(1)} custom-call(bf16[32,2048]{1,0:T(8,128)(2,1)S(1)} %copy-done.1, bf16[1024,2048]{1,0:T(8,128)(2,1)S(1)} %copy-done, s32[8]{0:T(128)S(1)} %copy-done.2, f32[9,8]{1,0:T(8,128)S(1)} %copy.6.ker_ref, f32[8]{0:T(128)S(1)} %copy-done.3), custom_call_target="tpu_custom_call" | custom-call | flops 8589934592 | bytes 5242880 | tf_op jit(solution)/shard_map/pallas_call | solution.py:376
  95.5 0.6 copy.8
Async XLA Ops:
  0.8 2.2 %copy-start = (bf16[1024,2048]{1,0:T(8,128)(2,1)S(1)}, bf16[1024,2048]{1,0:T(8,128)(2,1)}, u32[]{:S(2)}) copy-start(bf16[1024,2048]{1,0:T(8,128)(2,1)} %r_ref.1) | copy-start | bytes 12582916
  3.0 0.9 copy-start.1
  3.9 0.7 copy-start.2
  4.5 0.7 copy-start.3

commit v2 on v1

--- a/solution.py
+++ b/solution.py
@@ -19,6 +19,8 @@
 PLANE = NX * NY
 LANES = WIN * ROWS
 FLOOR = -1e30
+SCALE = 256.0 / S
+SCALE_2 = SCALE * 1.4426950408889634
 MESH = pl.DeviceIdType.MESH
 
 
@@ -190,14 +192,14 @@
 
     def score(w, zb, slot):
         queries = g[w, zb].reshape(2 * LANES, S)
+        group = lax.dot_general(
+            refs[w], queries, (((1,), (1,)), ((), ())), preferred_element_type=jnp.float32)
         peaks, totals = [], []
         for b in range(NB):
-            scores = lax.dot_general(
-                refs[w, b * BLOCK:(b + 1) * BLOCK, :], queries, (((1,), (1,)), ((), ())),
-                preferred_element_type=jnp.float32)
+            scores = group[b * BLOCK:(b + 1) * BLOCK]
             peak = jnp.max(scores, axis=0, keepdims=True)
-            totals.append(jnp.sum(jnp.exp((scores - peak) * (256.0 / S)), axis=0, keepdims=True))
-            peaks.append(peak * (256.0 / S))
+            totals.append(jnp.sum(jnp.exp2((scores - peak) * SCALE_2), axis=0, keepdims=True))
+            peaks.append(peak * SCALE)
         shifted = [peaks[b] + pen[b] for b in range(NB)]
         top = functools.reduce(jnp.maximum, shifted)
         total = functools.reduce(
@@ -337,7 +339,7 @@
             value = jnp.where(rows == a, read(a), value)
         return value
 
-    taps = [column(lambda a, t=t: ker_ref[t, a]) for t in range(TAPS)]
+    taps = [column(lambda a, t=t: ker_ref[a, t]) for t in range(TAPS)]
     bias = column(lambda a: bias_ref[a])
     recv(("h", 0), halo.at[0])
     recv(("h", 1), halo.at[1])
@@ -394,11 +396,11 @@
             pltpu.SemaphoreType.DMA((2 * WIN,)),
         ],
         compiler_params=pltpu.CompilerParams(
-            collective_id=0, has_side_effects=True, vmem_limit_bytes=48 * 1024 * 1024),
+            collective_id=0, has_side_effects=True, vmem_limit_bytes=60 * 1024 * 1024),
         cost_estimate=pl.CostEstimate(
             flops=2 * 2048 * REFS * S * WIN, bytes_accessed=5 * 1024 * 1024,
             transcendentals=2048 * REFS * WIN),
-    )(queries, references, labels, kernel, class_bias)
+    )(queries, references, labels, kernel.T, class_bias)
 
 
 def solution(mesh):

time: 96.2 us -> 82.7 us (0.86)
  Pallas kernels: 90.3 us -> 81.1 us
  local copies, waits for them, and re-layouts: 5.78 us -> 1.32 us
    pallas_call x1, Pallas kernels: 90.3 us -> 81.1 us  [per_device(): pl.pallas_call(functools.partial(body, ids), out_shape=jax.ShapeDtypeStru...]
    unnamed x10 -> x1, local copies, waits for them, and re-layouts: 5.78 us -> 1.32 us
where the time goes in v2:
time: 82.7 us; the launch traced here: 82.5 us
  Pallas kernels  81.1 us (98%)
  local copies, waits for them, and re-layouts  1.32 us (2%)
    pallas_call x1, Pallas kernels, per_device(): pl.pallas_call(functools.partial(body, ids), out_shape=jax.ShapeDtypeStru...  81.1 us

profile of v2, /device:TPU:1, one launch (start us, length us, event | category | flops | bytes accessed | tf_op | source)
XLA Modules:
  0.0 82.5 jit_solution(2534788641749444272)
XLA Ops:
  0.0 81.1 %shard_map.55 = f32[4,8,32]{2,1,0:T(8,128)} custom-call(bf16[32,2048]{1,0:T(8,128)(2,1)} %q_ref.1, bf16[1024,2048]{1,0:T(8,128)(2,1)} %r_ref.1, s32[8]{0:T(128)} %lab_ref.1, f32[8,9]{1,0:T(8,128)} %bitcast.1, f32[8]{0:T(128)} %bias_ref.1), custom_call_target="tpu_custom_call" | custom-call | flops 8589934592 | bytes 5242880 | tf_op jit(solution)/shard_map/pallas_call | solution.py:378
  81.1 1.3 %copy.7 = f32[4,8,32]{2,1,0:T(8,128)} copy(f32[4,8,32]{2,1,0:T(8,128)} %shard_map.55) | data formatting | bytes 8192

commit v3 on v2

--- a/solution.py
+++ b/solution.py
@@ -19,6 +19,7 @@
 PLANE = NX * NY
 LANES = WIN * ROWS
 FLOOR = -1e30
+EXACT = jnp.float8_e4m3fn
 SCALE = 256.0 / S
 SCALE_2 = SCALE * 1.4426950408889634
 MESH = pl.DeviceIdType.MESH
@@ -39,7 +40,7 @@
 
 
 def body(ids, q_ref, r_ref, lab_ref, ker_ref, bias_ref, out_ref,
-         g, refs, pen, part, sbuf, r1, zbuf, r2, cent, halo, ssem, rsem, lsem):
+         g, refs, pen, part, sbuf, r1, zbuf, r2, cent, halo, refs8, ssem, rsem, lsem):
     ref = lax.axis_index("ref")
     win = lax.axis_index("win")
     z, y, x = ref // PLANE, (ref // NX) % NY, ref % NX
@@ -191,9 +192,9 @@
         recv((kind, k, s), parts[kind](k, s))
 
     def score(w, zb, slot):
-        queries = g[w, zb].reshape(2 * LANES, S)
+        queries = g[w, zb].reshape(2 * LANES, S).astype(EXACT)
         group = lax.dot_general(
-            refs[w], queries, (((1,), (1,)), ((), ())), preferred_element_type=jnp.float32)
+            refs8[w], queries, (((1,), (1,)), ((), ())), preferred_element_type=jnp.float32)
         peaks, totals = [], []
         for b in range(NB):
             scores = group[b * BLOCK:(b + 1) * BLOCK]
@@ -269,6 +270,12 @@
         y_start(s)
     for copy in local[WIN:]:
         copy.wait()
+    def narrow(i, carry):
+        rows = pl.ds((i % WIN) * (REFS // WIN), REFS // WIN)
+        refs8[i // WIN, rows] = refs[i // WIN, rows].astype(EXACT)
+        return carry
+
+    lax.fori_loop(0, WIN * WIN, narrow, 0)
     stages[0][1]()
     compute(0, 0, 2)
     for s in signs:
@@ -391,6 +398,7 @@
             pltpu.VMEM((NZ, A, LANES), jnp.float32),
             pltpu.VMEM((A, LANES), jnp.float32),
             pltpu.VMEM((2, A, LANES), jnp.float32),
+            pltpu.VMEM((WIN, REFS, S), EXACT),
             pltpu.SemaphoreType.DMA((MESSAGES,)),
             pltpu.SemaphoreType.DMA((MESSAGES,)),
             pltpu.SemaphoreType.DMA((2 * WIN,)),

time: 82.7 us -> 81.8 us (0.989)
    pallas_call x1, Pallas kernels: 81.1 us -> 80.3 us  [per_device(): pl.pallas_call(functools.partial(body, ids), out_shape=jax.ShapeDtypeStru...]
where the time goes in v3:
time: 81.8 us; the launch traced here: 81.6 us
  Pallas kernels  80.3 us (98%)
  local copies, waits for them, and re-layouts  1.32 us (2%)
    pallas_call x1, Pallas kernels, per_device(): pl.pallas_call(functools.partial(body, ids), out_shape=jax.ShapeDtypeStru...  80.3 us

profile of v3, /device:TPU:1, one launch (start us, length us, event | category | flops | bytes accessed | tf_op | source)
XLA Modules:
  0.0 81.6 jit_solution(4282604718190786113)
XLA Ops:
  0.0 80.3 %shard_map.55 = f32[4,8,32]{2,1,0:T(8,128)} custom-call(bf16[32,2048]{1,0:T(8,128)(2,1)} %q_ref.1, bf16[1024,2048]{1,0:T(8,128)(2,1)} %r_ref.1, s32[8]{0:T(128)} %lab_ref.1, f32[8,9]{1,0:T(8,128)} %bitcast.1, f32[8]{0:T(128)} %bias_ref.1), custom_call_target="tpu_custom_call" | custom-call | flops 8589934592 | bytes 5242880 | tf_op jit(solution)/shard_map/pallas_call | solution.py:385
  80.3 1.3 %copy.7 = f32[4,8,32]{2,1,0:T(8,128)} copy(f32[4,8,32]{2,1,0:T(8,128)} %shard_map.55) | data formatting | bytes 8192
